TPU v7x, 128 devices: a whole 4x4x4 slice. The times are simulated.
128 devices in a mesh: grp: 4 (over x), row: 32 (over y, z, core).
Axes of the slice: x: 4, y: 4, z: 4, core: 2. Of those that a mesh axis runs over, the one named last changes fastest.
Arguments:
- matrix_tiles: float32 [512, 32, 128, 128], P(('grp', 'row')), may hold values from -2 to 2, as said below
- column_index: int32 [512, 32], P(('grp', 'row')), may hold values from 0 to 511, as said below
- precond: float32 [512, 128, 128], P(('grp', 'row')), may hold values from -12 to 16, as said below
- right_side: float32 [512, 16, 128], P(('grp', 'row')), may hold values from -60 to 60
- lost_group: int32 [1], replicated, may hold values from 0 to 16383
Outputs:
- recovered: float32 [512, 16, 128], P(('grp', 'row'))
- true_residual: float32 [512, 16, 128], P(('grp', 'row'))
Inputs may be any that keep to these rules, and one draw needn't show every extreme that they name: `column_index`: entry 0 of block row i is i; entry 1 is i + 12, or i - 12 where i + 12 passes the end; every entry lies within 12 of its block row. `precond`: every block is symmetric positive definite. `matrix_tiles`: the diagonal tile of each block row is near the identity.
All inputs are finite; a program needn't handle non-finite values.
Results may differ from a plain program's by a relative error of at most 0.0003.
Values sent between devices are 32-bit elements; how exact they have to be, the bound alone decides.
A program may use at most 64 MiB of HBM per device.

v0:
```python
import jax
import jax.numpy as jnp
from jax import lax
from jax.sharding import PartitionSpec as P

REACH = 3
OUTER = 2
INNER = 2
BAND = 12


def from_behind(value, axis, steps):
    count = lax.axis_size(axis)
    first, last = (max(0, -steps), min(count, count - steps))
    return lax.ppermute(value, axis, [(source, source + steps) for source in range(first, last)])


def inner_products(former, latter):
    return jnp.einsum("ica,ida->cd", former, latter, precision=lax.Precision.HIGHEST)


def scaled_by(vector, coeffs):
    return jnp.einsum("ica,cd->ida", vector, coeffs, precision=lax.Precision.HIGHEST)


def solve_sym(matrix, target):
    factor = jnp.linalg.cholesky(0.5 * (matrix + matrix.T))
    middle = lax.linalg.triangular_solve(factor, target, left_side=True, lower=True)
    return lax.linalg.triangular_solve(factor, middle, left_side=True, lower=True, transpose_a=True)


def neighbour(vector, offset):
    return from_behind(vector, ("grp", "row"), offset)


def group_neighbour(vector, offset):
    return from_behind(vector, "row", offset)


def window_of(vector, shifter):
    pieces = [shifter(vector, offset) for offset in range(REACH, 0, -1)]
    pieces.append(vector)
    for offset in range(1, REACH + 1):
        pieces.append(shifter(vector, -offset))
    return jnp.concatenate(pieces, 0)


def tile_product(matrix_tiles, window, local_cols, kept_mask):
    picked = jnp.take(window, local_cols, axis=0)
    if kept_mask is not None:
        picked = picked * kept_mask[:, :, None, None]
    return jnp.einsum("ikab,ikcb->ica", matrix_tiles, picked, precision=lax.Precision.HIGHEST)


def per_device(matrix_tiles, column_index, precond, right_side, lost_group):
    blocks = right_side.shape[0]
    row_count = lax.axis_size("row")
    group_count = lax.axis_size("grp")
    group_blocks = blocks * row_count
    my_group = lax.axis_index("grp")
    my_start = lax.axis_index(("grp", "row")) * blocks
    local_cols = column_index - (my_start - BAND)
    other_mask = (column_index // group_blocks != my_group).astype(jnp.float32)
    own_mask = 1.0 - other_mask
    lost = lost_group[0] % group_count

    def full_product(vector):
        return tile_product(matrix_tiles, window_of(vector, neighbour), local_cols, None)

    solution = jnp.zeros_like(right_side)
    residual = right_side
    direction = right_side
    squares = lax.psum(inner_products(residual, residual), ("grp", "row"))
    for outer_step in range(OUTER):
        applied = full_product(direction)
        curvature = lax.psum(inner_products(direction, applied), ("grp", "row"))
        advance = solve_sym(curvature, squares)
        solution = solution + scaled_by(direction, advance)
        residual = residual - scaled_by(applied, advance)
        squares_next = lax.psum(inner_products(residual, residual), ("grp", "row"))
        mixing = solve_sym(squares, squares_next)
        direction = residual + scaled_by(direction, mixing)
        squares = squares_next
    coupled = tile_product(matrix_tiles, window_of(solution, neighbour), local_cols, other_mask)
    inner_target = right_side - coupled

    def condition(vector):
        return jnp.einsum("iab,icb->ica", precond, vector, precision=lax.Precision.HIGHEST)

    estimate = jnp.zeros_like(inner_target)
    remainder = inner_target
    smoothed = condition(remainder)
    heading = smoothed
    weight = lax.psum(inner_products(remainder, smoothed), "row")
    for inner_step in range(INNER):
        applied = tile_product(
            matrix_tiles, window_of(heading, group_neighbour), local_cols, own_mask
        )
        bending = lax.psum(inner_products(heading, applied), "row")
        advance = solve_sym(bending, weight)
        estimate = estimate + scaled_by(heading, advance)
        remainder = remainder - scaled_by(applied, advance)
        if inner_step + 1 < INNER:
            smoothed = condition(remainder)
            weight_next = lax.psum(inner_products(remainder, smoothed), "row")
            heading = smoothed + scaled_by(heading, solve_sym(weight, weight_next))
            weight = weight_next
    recovered = jnp.where(my_group == lost, estimate, solution)
    true_residual = right_side - full_product(recovered)
    return (recovered, true_residual)


def solution(mesh):
    in_specs = (
        P(("grp", "row"), None, None, None),
        P(("grp", "row"), None),
        P(("grp", "row"), None, None),
        P(("grp", "row"), None, None),
        P(),
    )
    out_specs = (P(("grp", "row"), None, None), P(("grp", "row"), None, None))
    return jax.shard_map(
        per_device, mesh=mesh, in_specs=in_specs, out_specs=out_specs, check_vma=False
    )
```

profile of v0, /device:TPU:3, one launch (start us, length us, event | category | flops | bytes accessed | tf_op | source)
XLA Modules:
  0.0 685.8 jit_solution(15861666429005932232)
XLA Ops:
  0.6 8.8 %collective-permute-start.5 = (f32[4,16,128]{2,1,0:T(8,128)}, f32[4,16,128]{2,1,0:T(8,128)S(1)}, u32[]{:S(2)}, u32[]{:S(2)}) collective-permute-start(f32[4,16,128]{2,1,0:T(8,128)} %param.15), channel_id=1, source_target_pairs={{3,0},{4,1},{5,2},{6,3},{7,4},{8,5},{9,6},{10,7},{11,8},{12,9},{13... | collective-permute-start | bytes 98312 | tf_op jit(solution)/shard_map/ppermute | solution.py:15
  22.4 4.3 collective-permute-done
  28.7 7.4 %collective-permute-done.1 = f32[4,16,128]{2,1,0:T(8,128)S(1)} collective-permute-done((f32[4,16,128]{2,1,0:T(8,128)}, f32[4,16,128]{2,1,0:T(8,128)S(1)}, u32[]{:S(2)}, u32[]{:S(2)}) %collective-permute-start.1) | collective-permute-done | bytes 32800 | tf_op jit(solution)/shard_map/ppermute | solution.py:15
  37.7 9.4 %convolution_bitcast_fusion.9 = f32[4,16,128]{2,1,0:T(8,128)S(1)} fusion(f32[4,32,128,128]{3,2,1,0:T(8,128)} %param.12, f32[4,32,16,128]{3,2,1,0:T(8,128)S(1)} %bitcast.246, pred[4,32]{1,0:T(4,128)(4,1)S(1)} %get-tuple-element.12), kind=kOutput, calls=%fused_computation.26 | convolution fusion | flops 402915328 | bytes 9470080 | tf_op jit(solution)/shard_map/ikab,ikcb->ica/dot_general | solution.py:52
  47.2 62.8 %all-reduce = (f32[16,16]{1,0:T(8,128)S(1)}, f32[16,16]{1,0:T(8,128)S(1)}) all-reduce(f32[16,16]{1,0:T(8,128)S(1)} %convolution_bitcast_fusion.22, f32[16,16]{1,0:T(8,128)S(1)} %convolution_bitcast_fusion.23), channel_id=1, replica_groups=mesh['grp'=4,'row'=32] {'grp','row'}, use_global_device_ids=true, to_apply=%region_3.6 | all-reduce | flops 512 | bytes 4096 | tf_op jit(solution)/shard_map/psum | solution.py:73
  119.1 64.1 %psum.58 = f32[16,16]{1,0:T(8,128)S(1)} all-reduce(f32[16,16]{1,0:T(8,128)S(1)} %convolution_bitcast_fusion.20), channel_id=1, replica_groups=mesh['grp'=4,'row'=32] {'grp','row'}, use_global_device_ids=true, to_apply=%region_4.9 | all-reduce | flops 256 | bytes 2048 | tf_op jit(solution)/shard_map/psum | solution.py:80
  187.8 5.9 collective-permute-start.11
  204.6 6.5 collective-permute-done.7
  212.0 9.4 %convolution_bitcast_fusion.6 = f32[4,16,128]{2,1,0:T(8,128)S(1)} fusion(f32[4,32,128,128]{3,2,1,0:T(8,128)} %param.12, f32[4,32,16,128]{3,2,1,0:T(8,128)S(1)} %bitcast.247, pred[4,32]{1,0:T(4,128)(4,1)S(1)} %get-tuple-element.12), kind=kOutput, calls=%fused_computation.21 | convolution fusion | flops 402915328 | bytes 9470080 | tf_op jit(solution)/shard_map/ikab,ikcb->ica/dot_general | solution.py:52
  221.5 62.4 %psum.59 = f32[16,16]{1,0:T(8,128)S(1)} all-reduce(f32[16,16]{1,0:T(8,128)S(1)} %convolution_bitcast_fusion.18), channel_id=1, replica_groups=mesh['grp'=4,'row'=32] {'grp','row'}, use_global_device_ids=true, to_apply=%region_5.10 | all-reduce | flops 256 | bytes 2048 | tf_op jit(solution)/shard_map/psum | solution.py:76
  292.9 6.3 collective-permute-start.17
  310.3 6.1 collective-permute-done.13
  317.3 9.4 %fusion.5 = f32[4,16,128]{2,1,0:T(8,128)S(1)} fusion(f32[4,16,128]{2,1,0:T(8,128)S(1)} %copy-done.1, f32[4,32,128,128]{3,2,1,0:T(8,128)} %param.12, f32[4,32,16,128]{3,2,1,0:T(8,128)S(1)} %bitcast.242, f32[4,32]{1,0:T(4,128)S(1)} %get-tuple-element.11, pred[4,32]{1,0:T(4,128)(4,1)S(1)} %get-tuple-element.12), kind=kOutput, calls=%fused_computation.18 | convolution fusion | flops 403185664 | bytes 9503360 | tf_op jit(solution)/shard_map/ikab,ikcb->ica/dot_general | solution.py:52
  334.7 4.2 collective-permute-start.20
  344.7 9.4 %convolution_bitcast_fusion.4 = f32[4,16,128]{2,1,0:T(8,128)S(1)} fusion(f32[4,32,128,128]{3,2,1,0:T(8,128)} %param.12, f32[4,32,16,128]{3,2,1,0:T(8,128)S(1)} %bitcast.243, f32[4,32]{1,0:T(4,128)S(1)} %get-tuple-element.10, pred[4,32]{1,0:T(4,128)(4,1)S(1)} %get-tuple-element.12), kind=kOutput, calls=%fused_computation.16 | convolution fusion | flops 403177472 | bytes 9470592 | tf_op jit(solution)/shard_map/ikab,ikcb->ica/dot_general | solution.py:52
  354.3 119.3 %all-reduce.1 = (f32[16,16]{1,0:T(8,128)S(1)}, f32[16,16]{1,0:T(8,128)S(1)}) all-reduce(f32[16,16]{1,0:T(8,128)S(1)} %convolution_bitcast_fusion.15, f32[16,16]{1,0:T(8,128)S(1)} %convolution_bitcast_fusion.16), channel_id=1, replica_groups=mesh['grp'=4,'row'=32] {'row'}, use_global_device_ids=true, to_apply=%region_7.12 | all-reduce | flops 512 | bytes 4096 | tf_op jit(solution)/shard_map/psum | solution.py:94
  483.2 68.7 %psum.62 = f32[16,16]{1,0:T(8,128)S(1)} all-reduce(f32[16,16]{1,0:T(8,128)S(1)} %convolution_bitcast_fusion.13), channel_id=1, replica_groups=mesh['grp'=4,'row'=32] {'row'}, use_global_device_ids=true, to_apply=%region_8.13 | all-reduce | flops 256 | bytes 2048 | tf_op jit(solution)/shard_map/psum | solution.py:105
  563.3 4.2 collective-permute-start.25
  569.1 9.4 %convolution_bitcast_fusion.1 = f32[4,16,128]{2,1,0:T(8,128)S(1)} fusion(f32[4,32,128,128]{3,2,1,0:T(8,128)} %param.12, f32[4,32,16,128]{3,2,1,0:T(8,128)S(1)} %bitcast.244, f32[4,32]{1,0:T(4,128)S(1)} %get-tuple-element.10, pred[4,32]{1,0:T(4,128)(4,1)S(1)} %get-tuple-element.12), kind=kOutput, calls=%fused_computation.11 | convolution fusion | flops 403177472 | bytes 9470592 | tf_op jit(solution)/shard_map/ikab,ikcb->ica/dot_general | solution.py:52
  578.7 62.6 %psum.63 = f32[16,16]{1,0:T(8,128)S(1)} all-reduce(f32[16,16]{1,0:T(8,128)S(1)} %convolution_bitcast_fusion.11), channel_id=1, replica_groups=mesh['grp'=4,'row'=32] {'row'}, use_global_device_ids=true, to_apply=%region_9.14 | all-reduce | flops 256 | bytes 2048 | tf_op jit(solution)/shard_map/psum | solution.py:99
  648.1 7.9 %collective-permute-start.35 = (f32[4,16,128]{2,1,0:T(8,128)S(1)}, f32[4,16,128]{2,1,0:T(8,128)S(1)}, u32[]{:S(2)}, u32[]{:S(2)}) collective-permute-start(f32[4,16,128]{2,1,0:T(8,128)S(1)} %fusion.2), channel_id=1, source_target_pairs={{3,0},{4,1},{5,2},{6,3},{7,4},{8,5},{9,6},{10,7},{11,8},{12,9},{13... | collective-permute-start | bytes 98312 | tf_op jit(solution)/shard_map/ppermute | solution.py:15
  657.9 4.7 collective-permute-start.33
  668.1 6.8 collective-permute-done.31
  675.8 10.0 %fusion = f32[4,16,128]{2,1,0:T(8,128)} fusion(f32[4,16,128]{2,1,0:T(8,128)S(1)} %copy-done.1, f32[4,32,128,128]{3,2,1,0:T(8,128)} %param.12, f32[4,32,16,128]{3,2,1,0:T(8,128)S(1)} %bitcast.245, pred[4,32]{1,0:T(4,128)(4,1)S(1)} %get-tuple-element.12), kind=kOutput, calls=%fused_computation.7 | convolution fusion | flops 402923520 | bytes 9502848 | tf_op jit(solution)/shard_map/ikab,ikcb->ica/dot_general | solution.py:52
  (203 shorter events, 113.7 us)
Async XLA Ops:
  0.6 36.2 %collective-permute-start.5 = (f32[4,16,128]{2,1,0:T(8,128)}, f32[4,16,128]{2,1,0:T(8,128)S(1)}, u32[]{:S(2)}, u32[]{:S(2)}) collective-permute-start(f32[4,16,128]{2,1,0:T(8,128)} %param.15), channel_id=1, source_target_pairs={{3,0},{4,1},{5,2},{6,3},{7,4},{8,5},{9,6},{10,7},{11,8},{12,9},{13... | collective-permute-start | bytes 98312 | tf_op jit(solution)/shard_map/ppermute | solution.py:15
  9.4 27.4 %collective-permute-start.4 = (f32[4,16,128]{2,1,0:T(8,128)}, f32[4,16,128]{2,1,0:T(8,128)S(1)}, u32[]{:S(2)}, u32[]{:S(2)}) collective-permute-start(f32[4,16,128]{2,1,0:T(8,128)} %param.15), channel_id=1, source_target_pairs={{2,0},{3,1},{4,2},{5,3},{6,4},{7,5},{8,6},{9,7},{10,8},{11,9},{12,... | collective-permute-start | bytes 98312 | tf_op jit(solution)/shard_map/ppermute | solution.py:15
  11.5 25.4 %collective-permute-start.3 = (f32[4,16,128]{2,1,0:T(8,128)}, f32[4,16,128]{2,1,0:T(8,128)S(1)}, u32[]{:S(2)}, u32[]{:S(2)}) collective-permute-start(f32[4,16,128]{2,1,0:T(8,128)} %param.15), channel_id=1, source_target_pairs={{1,0},{2,1},{3,2},{4,3},{5,4},{6,5},{7,6},{8,7},{9,8},{10,9},{11,1... | collective-permute-start | bytes 98312 | tf_op jit(solution)/shard_map/ppermute | solution.py:15
  13.7 22.4 %collective-permute-start.2 = (f32[4,16,128]{2,1,0:T(8,128)}, f32[4,16,128]{2,1,0:T(8,128)S(1)}, u32[]{:S(2)}, u32[]{:S(2)}) collective-permute-start(f32[4,16,128]{2,1,0:T(8,128)} %param.15), channel_id=1, source_target_pairs={{0,1},{1,2},{2,3},{3,4},{4,5},{5,6},{6,7},{7,8},{8,9},{9,10},{10,1... | collective-permute-start | bytes 98312 | tf_op jit(solution)/shard_map/ppermute | solution.py:15
  183.8 18.4 %collective-permute-start.6 = (f32[4,16,128]{2,1,0:T(8,128)S(1)}, f32[4,16,128]{2,1,0:T(8,128)S(1)}, u32[]{:S(2)}, u32[]{:S(2)}) collective-permute-start(f32[4,16,128]{2,1,0:T(8,128)S(1)} %fusion.7), channel_id=1, source_target_pairs={{0,3},{1,4},{2,5},{3,6},{4,7},{5,8},{6,9},{7,10},{8,11},{9,12},{10... | collective-permute-start | bytes 98312 | tf_op jit(solution)/shard_map/ppermute | solution.py:15
  187.8 23.4 %collective-permute-start.11 = (f32[4,16,128]{2,1,0:T(8,128)S(1)}, f32[4,16,128]{2,1,0:T(8,128)S(1)}, u32[]{:S(2)}, u32[]{:S(2)}) collective-permute-start(f32[4,16,128]{2,1,0:T(8,128)S(1)} %fusion.7), channel_id=1, source_target_pairs={{3,0},{4,1},{5,2},{6,3},{7,4},{8,5},{9,6},{10,7},{11,8},{12,9},{13... | collective-permute-start | bytes 98312 | tf_op jit(solution)/shard_map/ppermute | solution.py:15
  193.7 17.4 %collective-permute-start.10 = (f32[4,16,128]{2,1,0:T(8,128)S(1)}, f32[4,16,128]{2,1,0:T(8,128)S(1)}, u32[]{:S(2)}, u32[]{:S(2)}) collective-permute-start(f32[4,16,128]{2,1,0:T(8,128)S(1)} %fusion.7), channel_id=1, source_target_pairs={{2,0},{3,1},{4,2},{5,3},{6,4},{7,5},{8,6},{9,7},{10,8},{11,9},{12,... | collective-permute-start | bytes 98312 | tf_op jit(solution)/shard_map/ppermute | solution.py:15
  195.7 15.5 %collective-permute-start.9 = (f32[4,16,128]{2,1,0:T(8,128)S(1)}, f32[4,16,128]{2,1,0:T(8,128)S(1)}, u32[]{:S(2)}, u32[]{:S(2)}) collective-permute-start(f32[4,16,128]{2,1,0:T(8,128)S(1)} %fusion.7), channel_id=1, source_target_pairs={{1,0},{2,1},{3,2},{4,3},{5,4},{6,5},{7,6},{8,7},{9,8},{10,9},{11,1... | collective-permute-start | bytes 98312 | tf_op jit(solution)/shard_map/ppermute | solution.py:15
  198.7 12.4 %collective-permute-start.8 = (f32[4,16,128]{2,1,0:T(8,128)S(1)}, f32[4,16,128]{2,1,0:T(8,128)S(1)}, u32[]{:S(2)}, u32[]{:S(2)}) collective-permute-start(f32[4,16,128]{2,1,0:T(8,128)S(1)} %fusion.7), channel_id=1, source_target_pairs={{0,1},{1,2},{2,3},{3,4},{4,5},{5,6},{6,7},{7,8},{8,9},{9,10},{10,1... | collective-permute-start | bytes 98312 | tf_op jit(solution)/shard_map/ppermute | solution.py:15
  288.7 18.9 %collective-permute-start.12 = (f32[4,16,128]{2,1,0:T(8,128)S(1)}, f32[4,16,128]{2,1,0:T(8,128)S(1)}, u32[]{:S(2)}, u32[]{:S(2)}) collective-permute-start(f32[4,16,128]{2,1,0:T(8,128)S(1)} %fusion.6), channel_id=1, source_target_pairs={{0,3},{1,4},{2,5},{3,6},{4,7},{5,8},{6,9},{7,10},{8,11},{9,12},{10... | collective-permute-start | bytes 98312 | tf_op jit(solution)/shard_map/ppermute | solution.py:15
  292.9 23.6 %collective-permute-start.17 = (f32[4,16,128]{2,1,0:T(8,128)S(1)}, f32[4,16,128]{2,1,0:T(8,128)S(1)}, u32[]{:S(2)}, u32[]{:S(2)}) collective-permute-start(f32[4,16,128]{2,1,0:T(8,128)S(1)} %fusion.6), channel_id=1, source_target_pairs={{3,0},{4,1},{5,2},{6,3},{7,4},{8,5},{9,6},{10,7},{11,8},{12,9},{13... | collective-permute-start | bytes 98312 | tf_op jit(solution)/shard_map/ppermute | solution.py:15
  299.2 17.3 %collective-permute-start.16 = (f32[4,16,128]{2,1,0:T(8,128)S(1)}, f32[4,16,128]{2,1,0:T(8,128)S(1)}, u32[]{:S(2)}, u32[]{:S(2)}) collective-permute-start(f32[4,16,128]{2,1,0:T(8,128)S(1)} %fusion.6), channel_id=1, source_target_pairs={{2,0},{3,1},{4,2},{5,3},{6,4},{7,5},{8,6},{9,7},{10,8},{11,9},{12,... | collective-permute-start | bytes 98312 | tf_op jit(solution)/shard_map/ppermute | solution.py:15
  302.0 14.5 %collective-permute-start.15 = (f32[4,16,128]{2,1,0:T(8,128)S(1)}, f32[4,16,128]{2,1,0:T(8,128)S(1)}, u32[]{:S(2)}, u32[]{:S(2)}) collective-permute-start(f32[4,16,128]{2,1,0:T(8,128)S(1)} %fusion.6), channel_id=1, source_target_pairs={{1,0},{2,1},{3,2},{4,3},{5,4},{6,5},{7,6},{8,7},{9,8},{10,9},{11,1... | collective-permute-start | bytes 98312 | tf_op jit(solution)/shard_map/ppermute | solution.py:15
  328.7 15.3 %collective-permute-start.23 = (f32[4,16,128]{2,1,0:T(8,128)S(1)}, f32[4,16,128]{2,1,0:T(8,128)S(1)}, u32[]{:S(2)}, u32[]{:S(2)}) collective-permute-start(f32[4,16,128]{2,1,0:T(8,128)S(1)} %fusion.81), channel_id=1, source_target_pairs={{3,0},{4,1},{5,2},{6,3},{7,4},{8,5},{9,6},{10,7},{11,8},{12,9},{13... | collective-permute-start | bytes 98312 | tf_op jit(solution)/shard_map/ppermute | solution.py:15
  330.0 13.9 %collective-permute-start.22 = (f32[4,16,128]{2,1,0:T(8,128)S(1)}, f32[4,16,128]{2,1,0:T(8,128)S(1)}, u32[]{:S(2)}, u32[]{:S(2)}) collective-permute-start(f32[4,16,128]{2,1,0:T(8,128)S(1)} %fusion.81), channel_id=1, source_target_pairs={{2,0},{3,1},{4,2},{5,3},{6,4},{7,5},{8,6},{9,7},{10,8},{11,9},{12,... | collective-permute-start | bytes 98312 | tf_op jit(solution)/shard_map/ppermute | solution.py:15
  331.3 12.6 %collective-permute-start.21 = (f32[4,16,128]{2,1,0:T(8,128)S(1)}, f32[4,16,128]{2,1,0:T(8,128)S(1)}, u32[]{:S(2)}, u32[]{:S(2)}) collective-permute-start(f32[4,16,128]{2,1,0:T(8,128)S(1)} %fusion.81), channel_id=1, source_target_pairs={{1,0},{2,1},{3,2},{4,3},{5,4},{6,5},{7,6},{8,7},{9,8},{10,9},{11,1... | collective-permute-start | bytes 98312 | tf_op jit(solution)/shard_map/ppermute | solution.py:15
  553.9 14.5 %collective-permute-start.29 = (f32[4,16,128]{2,1,0:T(8,128)S(1)}, f32[4,16,128]{2,1,0:T(8,128)S(1)}, u32[]{:S(2)}, u32[]{:S(2)}) collective-permute-start(f32[4,16,128]{2,1,0:T(8,128)S(1)} %fusion.3), channel_id=1, source_target_pairs={{3,0},{4,1},{5,2},{6,3},{7,4},{8,5},{9,6},{10,7},{11,8},{12,9},{13... | collective-permute-start | bytes 98312 | tf_op jit(solution)/shard_map/ppermute | solution.py:15
  555.2 13.1 %collective-permute-start.28 = (f32[4,16,128]{2,1,0:T(8,128)S(1)}, f32[4,16,128]{2,1,0:T(8,128)S(1)}, u32[]{:S(2)}, u32[]{:S(2)}) collective-permute-start(f32[4,16,128]{2,1,0:T(8,128)S(1)} %fusion.3), channel_id=1, source_target_pairs={{2,0},{3,1},{4,2},{5,3},{6,4},{7,5},{8,6},{9,7},{10,8},{11,9},{12,... | collective-permute-start | bytes 98312 | tf_op jit(solution)/shard_map/ppermute | solution.py:15
  556.5 11.8 %collective-permute-start.27 = (f32[4,16,128]{2,1,0:T(8,128)S(1)}, f32[4,16,128]{2,1,0:T(8,128)S(1)}, u32[]{:S(2)}, u32[]{:S(2)}) collective-permute-start(f32[4,16,128]{2,1,0:T(8,128)S(1)} %fusion.3), channel_id=1, source_target_pairs={{1,0},{2,1},{3,2},{4,3},{5,4},{6,5},{7,6},{8,7},{9,8},{10,9},{11,1... | collective-permute-start | bytes 98312 | tf_op jit(solution)/shard_map/ppermute | solution.py:15
  646.1 19.9 %collective-permute-start.30 = (f32[4,16,128]{2,1,0:T(8,128)S(1)}, f32[4,16,128]{2,1,0:T(8,128)S(1)}, u32[]{:S(2)}, u32[]{:S(2)}) collective-permute-start(f32[4,16,128]{2,1,0:T(8,128)S(1)} %fusion.2), channel_id=1, source_target_pairs={{0,3},{1,4},{2,5},{3,6},{4,7},{5,8},{6,9},{7,10},{8,11},{9,12},{10... | collective-permute-start | bytes 98312 | tf_op jit(solution)/shard_map/ppermute | solution.py:15
  648.1 27.0 %collective-permute-start.35 = (f32[4,16,128]{2,1,0:T(8,128)S(1)}, f32[4,16,128]{2,1,0:T(8,128)S(1)}, u32[]{:S(2)}, u32[]{:S(2)}) collective-permute-start(f32[4,16,128]{2,1,0:T(8,128)S(1)} %fusion.2), channel_id=1, source_target_pairs={{3,0},{4,1},{5,2},{6,3},{7,4},{8,5},{9,6},{10,7},{11,8},{12,9},{13... | collective-permute-start | bytes 98312 | tf_op jit(solution)/shard_map/ppermute | solution.py:15
  655.9 19.1 %collective-permute-start.34 = (f32[4,16,128]{2,1,0:T(8,128)S(1)}, f32[4,16,128]{2,1,0:T(8,128)S(1)}, u32[]{:S(2)}, u32[]{:S(2)}) collective-permute-start(f32[4,16,128]{2,1,0:T(8,128)S(1)} %fusion.2), channel_id=1, source_target_pairs={{2,0},{3,1},{4,2},{5,3},{6,4},{7,5},{8,6},{9,7},{10,8},{11,9},{12,... | collective-permute-start | bytes 98312 | tf_op jit(solution)/shard_map/ppermute | solution.py:15
  657.9 17.1 %collective-permute-start.33 = (f32[4,16,128]{2,1,0:T(8,128)S(1)}, f32[4,16,128]{2,1,0:T(8,128)S(1)}, u32[]{:S(2)}, u32[]{:S(2)}) collective-permute-start(f32[4,16,128]{2,1,0:T(8,128)S(1)} %fusion.2), channel_id=1, source_target_pairs={{1,0},{2,1},{3,2},{4,3},{5,4},{6,5},{7,6},{8,7},{9,8},{10,9},{11,1... | collective-permute-start | bytes 98312 | tf_op jit(solution)/shard_map/ppermute | solution.py:15
  662.5 12.4 %collective-permute-start.32 = (f32[4,16,128]{2,1,0:T(8,128)S(1)}, f32[4,16,128]{2,1,0:T(8,128)S(1)}, u32[]{:S(2)}, u32[]{:S(2)}) collective-permute-start(f32[4,16,128]{2,1,0:T(8,128)S(1)} %fusion.2), channel_id=1, source_target_pairs={{0,1},{1,2},{2,3},{3,4},{4,5},{5,6},{6,7},{7,8},{8,9},{9,10},{10,1... | collective-permute-start | bytes 98312 | tf_op jit(solution)/shard_map/ppermute | solution.py:15
  (16 other events, 579.8 us)
where the time goes:
time: 687 us; the launch traced here: 686 us
  blocking collectives  440 us (64%)
  starting transfers between devices  116 us (17%)
  matrix products  63.8 us (9%)
  waiting for transfers between devices  32.9 us (5%)
  other arithmetic  24.9 us (4%)
    psum x1, blocking collectives, per_device(): weight = lax.psum(inner_products(remainder, smoothed), 'row')  119 us
    ppermute x36, starting transfers between devices, from_behind(): lax.ppermute(value, axis, [(source, source + steps) for source in range(f...  116 us
    psum x1, blocking collectives, per_device(): weight_next = lax.psum(inner_products(remainder, smoothed), 'row')  68.7 us
    psum x1, blocking collectives, per_device(): squares_next = lax.psum(inner_products(residual, residual), ('grp', 'row'))  64.1 us
    psum x1, blocking collectives, per_device(): squares = lax.psum(inner_products(residual, residual), ('grp', 'row'))  62.8 us
    psum x1, blocking collectives, per_device(): bending = lax.psum(inner_products(heading, applied), 'row')  62.6 us
    psum x1, blocking collectives, per_device(): curvature = lax.psum(inner_products(direction, applied), ('grp', 'row'))  62.4 us
    dot_general x6, matrix products, tile_product(): jnp.einsum('ikab,ikcb->ica', matrix_tiles, picked, precision=lax.Precisio...  57 us
  transfers between devices with their start and end apart: 36, of which 7 were waited for; matrix products, arithmetic and copies ran while one was open for 0% of the time, Pallas kernels for 0%

commit v1 on v0

--- a/solution.py
+++ b/solution.py
@@ -70,7 +70,7 @@
     solution = jnp.zeros_like(right_side)
     residual = right_side
     direction = right_side
-    squares = lax.psum(inner_products(residual, residual), ("grp", "row"))
+    squares = lax.psum(lax.psum(inner_products(residual, residual), "grp"), "row")
     for outer_step in range(OUTER):
         applied = full_product(direction)
         curvature = lax.psum(inner_products(direction, applied), ("grp", "row"))

time: 687 us -> 755 us (1.099)
  blocking collectives: 440 us -> 512 us
    psum x1 -> x2, blocking collectives: 62.4 us -> 128 us  [per_device(): curvature = lax.psum(inner_products(direction, applied), ('grp', 'row'))]
    psum x1 -> x2, blocking collectives: 62.8 us -> 71.8 us  [the longest x1 65.1 us: per_device(): lax.psum(lax.psum(inner_products(residual, residual), 'grp'), 'row')]
  transfers between devices with their start and end apart: 36 -> 36, of which waited for: 7 -> 6; matrix products, arithmetic and copies ran while one was open for 0% -> 1% of each run, Pallas kernels for 0% -> 0%
where the time goes in v1:
time: 755 us; the launch traced here: 753 us
  blocking collectives  512 us (68%)
  starting transfers between devices  114 us (15%)
  matrix products  63.8 us (8%)
  waiting for transfers between devices  29.5 us (4%)
  other arithmetic  24.9 us (3%)
    psum x2, blocking collectives, per_device(): curvature = lax.psum(inner_products(direction, applied), ('grp', 'row'))  128 us
    psum x1, blocking collectives, per_device(): weight = lax.psum(inner_products(remainder, smoothed), 'row')  119 us
    ppermute x36, starting transfers between devices, from_behind(): lax.ppermute(value, axis, [(source, source + steps) for source in range(f...  114 us
    psum x1, blocking collectives, per_device(): weight_next = lax.psum(inner_products(remainder, smoothed), 'row')  68.7 us
    psum x1, blocking collectives, per_device(): lax.psum(lax.psum(inner_products(residual, residual), 'grp'), 'row')  65.1 us
    psum x1, blocking collectives, per_device(): bending = lax.psum(inner_products(heading, applied), 'row')  62.6 us
    psum x1, blocking collectives, per_device(): squares_next = lax.psum(inner_products(residual, residual), ('grp', 'row'))  61.9 us
    dot_general x6, matrix products, tile_product(): jnp.einsum('ikab,ikcb->ica', matrix_tiles, picked, precision=lax.Precisio...  57 us
  transfers between devices with their start and end apart: 36, of which 6 were waited for; matrix products, arithmetic and copies ran while one was open for 1% of the time, Pallas kernels for 0%

profile of v1, /device:TPU:3, one launch (start us, length us, event | category | flops | bytes accessed | tf_op | source)
XLA Modules:
  0.0 753.2 jit_solution(1580384189595579685)
XLA Ops:
  0.6 8.8 %collective-permute-start.5 = (f32[4,16,128]{2,1,0:T(8,128)}, f32[4,16,128]{2,1,0:T(8,128)S(1)}, u32[]{:S(2)}, u32[]{:S(2)}) collective-permute-start(f32[4,16,128]{2,1,0:T(8,128)} %param.15), channel_id=1, source_target_pairs={{3,0},{4,1},{5,2},{6,3},{7,4},{8,5},{9,6},{10,7},{11,8},{12,9},{13... | collective-permute-start | bytes 98312 | tf_op jit(solution)/shard_map/ppermute | solution.py:15
  22.4 6.7 psum.64
  29.1 65.1 %psum.65 = f32[16,16]{1,0:T(8,128)S(1)} all-reduce(f32[16,16]{1,0:T(8,128)S(1)} %psum.64), channel_id=1, replica_groups=mesh['grp'=4,'row'=32] {'row'}, use_global_device_ids=true, to_apply=%region_4.7 | all-reduce | flops 256 | bytes 2048 | tf_op jit(solution)/shard_map/psum | solution.py:73
  100.3 7.1 collective-permute-done.1
  109.1 9.4 %convolution_bitcast_fusion.9 = f32[4,16,128]{2,1,0:T(8,128)S(1)} fusion(f32[4,32,128,128]{3,2,1,0:T(8,128)} %param.12, f32[4,32,16,128]{3,2,1,0:T(8,128)S(1)} %bitcast.246, pred[4,32]{1,0:T(4,128)(4,1)S(1)} %get-tuple-element.10), kind=kOutput, calls=%fused_computation.26 | convolution fusion | flops 402915328 | bytes 9470080 | tf_op jit(solution)/shard_map/ikab,ikcb->ica/dot_general | solution.py:52
  118.6 65.6 %psum.63 = f32[16,16]{1,0:T(8,128)S(1)} all-reduce(f32[16,16]{1,0:T(8,128)S(1)} %convolution_bitcast_fusion.23), channel_id=1, replica_groups=mesh['grp'=4,'row'=32] {'grp','row'}, use_global_device_ids=true, to_apply=%region_0.2 | all-reduce | flops 256 | bytes 2048 | tf_op jit(solution)/shard_map/psum | solution.py:76
  189.1 61.9 %psum.66 = f32[16,16]{1,0:T(8,128)S(1)} all-reduce(f32[16,16]{1,0:T(8,128)S(1)} %convolution_bitcast_fusion.20), channel_id=1, replica_groups=mesh['grp'=4,'row'=32] {'grp','row'}, use_global_device_ids=true, to_apply=%region_5.10 | all-reduce | flops 256 | bytes 2048 | tf_op jit(solution)/shard_map/psum | solution.py:80
  255.4 6.2 collective-permute-start.11
  272.5 6.8 collective-permute-done.7
  280.1 9.4 %convolution_bitcast_fusion.6 = f32[4,16,128]{2,1,0:T(8,128)S(1)} fusion(f32[4,32,128,128]{3,2,1,0:T(8,128)} %param.12, f32[4,32,16,128]{3,2,1,0:T(8,128)S(1)} %bitcast.247, pred[4,32]{1,0:T(4,128)(4,1)S(1)} %get-tuple-element.10), kind=kOutput, calls=%fused_computation.21 | convolution fusion | flops 402915328 | bytes 9470080 | tf_op jit(solution)/shard_map/ikab,ikcb->ica/dot_general | solution.py:52
  289.6 62.5 %psum.67 = f32[16,16]{1,0:T(8,128)S(1)} all-reduce(f32[16,16]{1,0:T(8,128)S(1)} %convolution_bitcast_fusion.18), channel_id=1, replica_groups=mesh['grp'=4,'row'=32] {'grp','row'}, use_global_device_ids=true, to_apply=%region_6.11 | all-reduce | flops 256 | bytes 2048 | tf_op jit(solution)/shard_map/psum | solution.py:76
  361.4 6.0 collective-permute-start.17
  378.3 6.9 collective-permute-done.13
  386.1 9.4 %fusion.5 = f32[4,16,128]{2,1,0:T(8,128)S(1)} fusion(f32[4,16,128]{2,1,0:T(8,128)S(1)} %copy-done.1, f32[4,32,128,128]{3,2,1,0:T(8,128)} %param.12, f32[4,32,16,128]{3,2,1,0:T(8,128)S(1)} %bitcast.242, f32[4,32]{1,0:T(4,128)S(1)} %get-tuple-element.9, pred[4,32]{1,0:T(4,128)(4,1)S(1)} %get-tuple-element.10), kind=kOutput, calls=%fused_computation.18 | convolution fusion | flops 403185664 | bytes 9503360 | tf_op jit(solution)/shard_map/ikab,ikcb->ica/dot_general | solution.py:52
  412.5 9.4 %convolution_bitcast_fusion.4 = f32[4,16,128]{2,1,0:T(8,128)S(1)} fusion(f32[4,32,128,128]{3,2,1,0:T(8,128)} %param.12, f32[4,32,16,128]{3,2,1,0:T(8,128)S(1)} %bitcast.243, f32[4,32]{1,0:T(4,128)S(1)} %get-tuple-element.8, pred[4,32]{1,0:T(4,128)(4,1)S(1)} %get-tuple-element.10), kind=kOutput, calls=%fused_computation.16 | convolution fusion | flops 403177472 | bytes 9470592 | tf_op jit(solution)/shard_map/ikab,ikcb->ica/dot_general | solution.py:52
  422.1 118.9 %all-reduce = (f32[16,16]{1,0:T(8,128)S(1)}, f32[16,16]{1,0:T(8,128)S(1)}) all-reduce(f32[16,16]{1,0:T(8,128)S(1)} %convolution_bitcast_fusion.15, f32[16,16]{1,0:T(8,128)S(1)} %convolution_bitcast_fusion.16), channel_id=1, replica_groups=mesh['grp'=4,'row'=32] {'row'}, use_global_device_ids=true, to_apply=%region_8.13 | all-reduce | flops 512 | bytes 4096 | tf_op jit(solution)/shard_map/psum | solution.py:94
  550.6 68.7 %psum.70 = f32[16,16]{1,0:T(8,128)S(1)} all-reduce(f32[16,16]{1,0:T(8,128)S(1)} %convolution_bitcast_fusion.13), channel_id=1, replica_groups=mesh['grp'=4,'row'=32] {'row'}, use_global_device_ids=true, to_apply=%region_9.14 | all-reduce | flops 256 | bytes 2048 | tf_op jit(solution)/shard_map/psum | solution.py:105
  630.7 4.2 collective-permute-start.25
  636.5 9.4 %convolution_bitcast_fusion.1 = f32[4,16,128]{2,1,0:T(8,128)S(1)} fusion(f32[4,32,128,128]{3,2,1,0:T(8,128)} %param.12, f32[4,32,16,128]{3,2,1,0:T(8,128)S(1)} %bitcast.244, f32[4,32]{1,0:T(4,128)S(1)} %get-tuple-element.8, pred[4,32]{1,0:T(4,128)(4,1)S(1)} %get-tuple-element.10), kind=kOutput, calls=%fused_computation.11 | convolution fusion | flops 403177472 | bytes 9470592 | tf_op jit(solution)/shard_map/ikab,ikcb->ica/dot_general | solution.py:52
  646.1 62.6 %psum.71 = f32[16,16]{1,0:T(8,128)S(1)} all-reduce(f32[16,16]{1,0:T(8,128)S(1)} %convolution_bitcast_fusion.11), channel_id=1, replica_groups=mesh['grp'=4,'row'=32] {'row'}, use_global_device_ids=true, to_apply=%region_10.15 | all-reduce | flops 256 | bytes 2048 | tf_op jit(solution)/shard_map/psum | solution.py:99
  715.5 7.9 %collective-permute-start.35 = (f32[4,16,128]{2,1,0:T(8,128)S(1)}, f32[4,16,128]{2,1,0:T(8,128)S(1)}, u32[]{:S(2)}, u32[]{:S(2)}) collective-permute-start(f32[4,16,128]{2,1,0:T(8,128)S(1)} %fusion.2), channel_id=1, source_target_pairs={{3,0},{4,1},{5,2},{6,3},{7,4},{8,5},{9,6},{10,7},{11,8},{12,9},{13... | collective-permute-start | bytes 98312 | tf_op jit(solution)/shard_map/ppermute | solution.py:15
  725.3 4.7 collective-permute-start.33
  735.5 6.8 collective-permute-done.31
  743.2 10.0 %fusion = f32[4,16,128]{2,1,0:T(8,128)} fusion(f32[4,16,128]{2,1,0:T(8,128)S(1)} %copy-done.1, f32[4,32,128,128]{3,2,1,0:T(8,128)} %param.12, f32[4,32,16,128]{3,2,1,0:T(8,128)S(1)} %bitcast.245, pred[4,32]{1,0:T(4,128)(4,1)S(1)} %get-tuple-element.10), kind=kOutput, calls=%fused_computation.7 | convolution fusion | flops 402923520 | bytes 9502848 | tf_op jit(solution)/shard_map/ikab,ikcb->ica/dot_general | solution.py:52
  (205 shorter events, 116.6 us)
Async XLA Ops:
  0.6 107.6 %collective-permute-start.5 = (f32[4,16,128]{2,1,0:T(8,128)}, f32[4,16,128]{2,1,0:T(8,128)S(1)}, u32[]{:S(2)}, u32[]{:S(2)}) collective-permute-start(f32[4,16,128]{2,1,0:T(8,128)} %param.15), channel_id=1, source_target_pairs={{3,0},{4,1},{5,2},{6,3},{7,4},{8,5},{9,6},{10,7},{11,8},{12,9},{13... | collective-permute-start | bytes 98312 | tf_op jit(solution)/shard_map/ppermute | solution.py:15
  9.4 98.8 %collective-permute-start.4 = (f32[4,16,128]{2,1,0:T(8,128)}, f32[4,16,128]{2,1,0:T(8,128)S(1)}, u32[]{:S(2)}, u32[]{:S(2)}) collective-permute-start(f32[4,16,128]{2,1,0:T(8,128)} %param.15), channel_id=1, source_target_pairs={{2,0},{3,1},{4,2},{5,3},{6,4},{7,5},{8,6},{9,7},{10,8},{11,9},{12,... | collective-permute-start | bytes 98312 | tf_op jit(solution)/shard_map/ppermute | solution.py:15
  11.5 96.8 %collective-permute-start.3 = (f32[4,16,128]{2,1,0:T(8,128)}, f32[4,16,128]{2,1,0:T(8,128)S(1)}, u32[]{:S(2)}, u32[]{:S(2)}) collective-permute-start(f32[4,16,128]{2,1,0:T(8,128)} %param.15), channel_id=1, source_target_pairs={{1,0},{2,1},{3,2},{4,3},{5,4},{6,5},{7,6},{8,7},{9,8},{10,9},{11,1... | collective-permute-start | bytes 98312 | tf_op jit(solution)/shard_map/ppermute | solution.py:15
  13.7 93.8 %collective-permute-start.2 = (f32[4,16,128]{2,1,0:T(8,128)}, f32[4,16,128]{2,1,0:T(8,128)S(1)}, u32[]{:S(2)}, u32[]{:S(2)}) collective-permute-start(f32[4,16,128]{2,1,0:T(8,128)} %param.15), channel_id=1, source_target_pairs={{0,1},{1,2},{2,3},{3,4},{4,5},{5,6},{6,7},{7,8},{8,9},{9,10},{10,1... | collective-permute-start | bytes 98312 | tf_op jit(solution)/shard_map/ppermute | solution.py:15
  17.1 81.3 %collective-permute-start = (f32[4,16,128]{2,1,0:T(8,128)}, f32[4,16,128]{2,1,0:T(8,128)S(1)}, u32[]{:S(2)}, u32[]{:S(2)}) collective-permute-start(f32[4,16,128]{2,1,0:T(8,128)} %param.15), channel_id=1, source_target_pairs={{0,3},{1,4},{2,5},{3,6},{4,7},{5,8},{6,9},{7,10},{8,11},{9,12},{10... | collective-permute-start | bytes 98312 | tf_op jit(solution)/shard_map/ppermute | solution.py:15
  251.6 18.3 %collective-permute-start.6 = (f32[4,16,128]{2,1,0:T(8,128)S(1)}, f32[4,16,128]{2,1,0:T(8,128)S(1)}, u32[]{:S(2)}, u32[]{:S(2)}) collective-permute-start(f32[4,16,128]{2,1,0:T(8,128)S(1)} %fusion.7), channel_id=1, source_target_pairs={{0,3},{1,4},{2,5},{3,6},{4,7},{5,8},{6,9},{7,10},{8,11},{9,12},{10... | collective-permute-start | bytes 98312 | tf_op jit(solution)/shard_map/ppermute | solution.py:15
  255.4 24.0 %collective-permute-start.11 = (f32[4,16,128]{2,1,0:T(8,128)S(1)}, f32[4,16,128]{2,1,0:T(8,128)S(1)}, u32[]{:S(2)}, u32[]{:S(2)}) collective-permute-start(f32[4,16,128]{2,1,0:T(8,128)S(1)} %fusion.7), channel_id=1, source_target_pairs={{3,0},{4,1},{5,2},{6,3},{7,4},{8,5},{9,6},{10,7},{11,8},{12,9},{13... | collective-permute-start | bytes 98312 | tf_op jit(solution)/shard_map/ppermute | solution.py:15
  261.6 17.7 %collective-permute-start.10 = (f32[4,16,128]{2,1,0:T(8,128)S(1)}, f32[4,16,128]{2,1,0:T(8,128)S(1)}, u32[]{:S(2)}, u32[]{:S(2)}) collective-permute-start(f32[4,16,128]{2,1,0:T(8,128)S(1)} %fusion.7), channel_id=1, source_target_pairs={{2,0},{3,1},{4,2},{5,3},{6,4},{7,5},{8,6},{9,7},{10,8},{11,9},{12,... | collective-permute-start | bytes 98312 | tf_op jit(solution)/shard_map/ppermute | solution.py:15
  264.0 15.3 %collective-permute-start.9 = (f32[4,16,128]{2,1,0:T(8,128)S(1)}, f32[4,16,128]{2,1,0:T(8,128)S(1)}, u32[]{:S(2)}, u32[]{:S(2)}) collective-permute-start(f32[4,16,128]{2,1,0:T(8,128)S(1)} %fusion.7), channel_id=1, source_target_pairs={{1,0},{2,1},{3,2},{4,3},{5,4},{6,5},{7,6},{8,7},{9,8},{10,9},{11,1... | collective-permute-start | bytes 98312 | tf_op jit(solution)/shard_map/ppermute | solution.py:15
  267.2 12.1 %collective-permute-start.8 = (f32[4,16,128]{2,1,0:T(8,128)S(1)}, f32[4,16,128]{2,1,0:T(8,128)S(1)}, u32[]{:S(2)}, u32[]{:S(2)}) collective-permute-start(f32[4,16,128]{2,1,0:T(8,128)S(1)} %fusion.7), channel_id=1, source_target_pairs={{0,1},{1,2},{2,3},{3,4},{4,5},{5,6},{6,7},{7,8},{8,9},{9,10},{10,1... | collective-permute-start | bytes 98312 | tf_op jit(solution)/shard_map/ppermute | solution.py:15
  356.9 18.8 %collective-permute-start.12 = (f32[4,16,128]{2,1,0:T(8,128)S(1)}, f32[4,16,128]{2,1,0:T(8,128)S(1)}, u32[]{:S(2)}, u32[]{:S(2)}) collective-permute-start(f32[4,16,128]{2,1,0:T(8,128)S(1)} %fusion.6), channel_id=1, source_target_pairs={{0,3},{1,4},{2,5},{3,6},{4,7},{5,8},{6,9},{7,10},{8,11},{9,12},{10... | collective-permute-start | bytes 98312 | tf_op jit(solution)/shard_map/ppermute | solution.py:15
  361.4 23.9 %collective-permute-start.17 = (f32[4,16,128]{2,1,0:T(8,128)S(1)}, f32[4,16,128]{2,1,0:T(8,128)S(1)}, u32[]{:S(2)}, u32[]{:S(2)}) collective-permute-start(f32[4,16,128]{2,1,0:T(8,128)S(1)} %fusion.6), channel_id=1, source_target_pairs={{3,0},{4,1},{5,2},{6,3},{7,4},{8,5},{9,6},{10,7},{11,8},{12,9},{13... | collective-permute-start | bytes 98312 | tf_op jit(solution)/shard_map/ppermute | solution.py:15
  367.4 17.9 %collective-permute-start.16 = (f32[4,16,128]{2,1,0:T(8,128)S(1)}, f32[4,16,128]{2,1,0:T(8,128)S(1)}, u32[]{:S(2)}, u32[]{:S(2)}) collective-permute-start(f32[4,16,128]{2,1,0:T(8,128)S(1)} %fusion.6), channel_id=1, source_target_pairs={{2,0},{3,1},{4,2},{5,3},{6,4},{7,5},{8,6},{9,7},{10,8},{11,9},{12,... | collective-permute-start | bytes 98312 | tf_op jit(solution)/shard_map/ppermute | solution.py:15
  369.4 15.9 %collective-permute-start.15 = (f32[4,16,128]{2,1,0:T(8,128)S(1)}, f32[4,16,128]{2,1,0:T(8,128)S(1)}, u32[]{:S(2)}, u32[]{:S(2)}) collective-permute-start(f32[4,16,128]{2,1,0:T(8,128)S(1)} %fusion.6), channel_id=1, source_target_pairs={{1,0},{2,1},{3,2},{4,3},{5,4},{6,5},{7,6},{8,7},{9,8},{10,9},{11,1... | collective-permute-start | bytes 98312 | tf_op jit(solution)/shard_map/ppermute | solution.py:15
  372.9 12.4 %collective-permute-start.14 = (f32[4,16,128]{2,1,0:T(8,128)S(1)}, f32[4,16,128]{2,1,0:T(8,128)S(1)}, u32[]{:S(2)}, u32[]{:S(2)}) collective-permute-start(f32[4,16,128]{2,1,0:T(8,128)S(1)} %fusion.6), channel_id=1, source_target_pairs={{0,1},{1,2},{2,3},{3,4},{4,5},{5,6},{6,7},{7,8},{8,9},{9,10},{10,1... | collective-permute-start | bytes 98312 | tf_op jit(solution)/shard_map/ppermute | solution.py:15
  397.5 14.2 %collective-permute-start.23 = (f32[4,16,128]{2,1,0:T(8,128)S(1)}, f32[4,16,128]{2,1,0:T(8,128)S(1)}, u32[]{:S(2)}, u32[]{:S(2)}) collective-permute-start(f32[4,16,128]{2,1,0:T(8,128)S(1)} %fusion.81), channel_id=1, source_target_pairs={{3,0},{4,1},{5,2},{6,3},{7,4},{8,5},{9,6},{10,7},{11,8},{12,9},{13... | collective-permute-start | bytes 98312 | tf_op jit(solution)/shard_map/ppermute | solution.py:15
  398.8 12.9 %collective-permute-start.22 = (f32[4,16,128]{2,1,0:T(8,128)S(1)}, f32[4,16,128]{2,1,0:T(8,128)S(1)}, u32[]{:S(2)}, u32[]{:S(2)}) collective-permute-start(f32[4,16,128]{2,1,0:T(8,128)S(1)} %fusion.81), channel_id=1, source_target_pairs={{2,0},{3,1},{4,2},{5,3},{6,4},{7,5},{8,6},{9,7},{10,8},{11,9},{12,... | collective-permute-start | bytes 98312 | tf_op jit(solution)/shard_map/ppermute | solution.py:15
  621.3 14.5 %collective-permute-start.29 = (f32[4,16,128]{2,1,0:T(8,128)S(1)}, f32[4,16,128]{2,1,0:T(8,128)S(1)}, u32[]{:S(2)}, u32[]{:S(2)}) collective-permute-start(f32[4,16,128]{2,1,0:T(8,128)S(1)} %fusion.3), channel_id=1, source_target_pairs={{3,0},{4,1},{5,2},{6,3},{7,4},{8,5},{9,6},{10,7},{11,8},{12,9},{13... | collective-permute-start | bytes 98312 | tf_op jit(solution)/shard_map/ppermute | solution.py:15
  622.6 13.1 %collective-permute-start.28 = (f32[4,16,128]{2,1,0:T(8,128)S(1)}, f32[4,16,128]{2,1,0:T(8,128)S(1)}, u32[]{:S(2)}, u32[]{:S(2)}) collective-permute-start(f32[4,16,128]{2,1,0:T(8,128)S(1)} %fusion.3), channel_id=1, source_target_pairs={{2,0},{3,1},{4,2},{5,3},{6,4},{7,5},{8,6},{9,7},{10,8},{11,9},{12,... | collective-permute-start | bytes 98312 | tf_op jit(solution)/shard_map/ppermute | solution.py:15
  713.5 19.9 %collective-permute-start.30 = (f32[4,16,128]{2,1,0:T(8,128)S(1)}, f32[4,16,128]{2,1,0:T(8,128)S(1)}, u32[]{:S(2)}, u32[]{:S(2)}) collective-permute-start(f32[4,16,128]{2,1,0:T(8,128)S(1)} %fusion.2), channel_id=1, source_target_pairs={{0,3},{1,4},{2,5},{3,6},{4,7},{5,8},{6,9},{7,10},{8,11},{9,12},{10... | collective-permute-start | bytes 98312 | tf_op jit(solution)/shard_map/ppermute | solution.py:15
  715.5 27.0 %collective-permute-start.35 = (f32[4,16,128]{2,1,0:T(8,128)S(1)}, f32[4,16,128]{2,1,0:T(8,128)S(1)}, u32[]{:S(2)}, u32[]{:S(2)}) collective-permute-start(f32[4,16,128]{2,1,0:T(8,128)S(1)} %fusion.2), channel_id=1, source_target_pairs={{3,0},{4,1},{5,2},{6,3},{7,4},{8,5},{9,6},{10,7},{11,8},{12,9},{13... | collective-permute-start | bytes 98312 | tf_op jit(solution)/shard_map/ppermute | solution.py:15
  723.3 19.1 %collective-permute-start.34 = (f32[4,16,128]{2,1,0:T(8,128)S(1)}, f32[4,16,128]{2,1,0:T(8,128)S(1)}, u32[]{:S(2)}, u32[]{:S(2)}) collective-permute-start(f32[4,16,128]{2,1,0:T(8,128)S(1)} %fusion.2), channel_id=1, source_target_pairs={{2,0},{3,1},{4,2},{5,3},{6,4},{7,5},{8,6},{9,7},{10,8},{11,9},{12,... | collective-permute-start | bytes 98312 | tf_op jit(solution)/shard_map/ppermute | solution.py:15
  725.3 17.1 %collective-permute-start.33 = (f32[4,16,128]{2,1,0:T(8,128)S(1)}, f32[4,16,128]{2,1,0:T(8,128)S(1)}, u32[]{:S(2)}, u32[]{:S(2)}) collective-permute-start(f32[4,16,128]{2,1,0:T(8,128)S(1)} %fusion.2), channel_id=1, source_target_pairs={{1,0},{2,1},{3,2},{4,3},{5,4},{6,5},{7,6},{8,7},{9,8},{10,9},{11,1... | collective-permute-start | bytes 98312 | tf_op jit(solution)/shard_map/ppermute | solution.py:15
  729.9 12.4 %collective-permute-start.32 = (f32[4,16,128]{2,1,0:T(8,128)S(1)}, f32[4,16,128]{2,1,0:T(8,128)S(1)}, u32[]{:S(2)}, u32[]{:S(2)}) collective-permute-start(f32[4,16,128]{2,1,0:T(8,128)S(1)} %fusion.2), channel_id=1, source_target_pairs={{0,1},{1,2},{2,3},{3,4},{4,5},{5,6},{6,7},{7,8},{8,9},{9,10},{10,1... | collective-permute-start | bytes 98312 | tf_op jit(solution)/shard_map/ppermute | solution.py:15
  (16 other events, 648.7 us)
